TPU v7x, 512 devices: a whole 4x8x8 slice. The times are simulated.
512 devices in a mesh: row: 8 (over z_hi, core), col: 8 (over z_lo, x), dep: 8 (over y).
Axes of the slice: x: 4, y: 8, z: 8 (z_hi: 4, z_lo: 2; z = z_hi * 2 + z_lo), core: 2. Of those that a mesh axis runs over, the one named last changes fastest.
Arguments:
- inputs: bfloat16 [4096, 6144], P(('row', 'dep'), 'col'), may hold values from -16 to 16
- weight: bfloat16 [6144, 24576], P(('col', 'row'), 'dep'), may hold values from -0.078125 to 0.078125
- grad_out: bfloat16 [4096, 24576], P(('row', 'col'), 'dep'), may hold values from -16 to 16
Outputs:
- hidden: bfloat16 [4096, 24576], P(('row', 'col'), 'dep')
- grad_inputs: bfloat16 [4096, 6144], P(('row', 'dep'), 'col')
All inputs are finite; a program needn't handle non-finite values.
Results may differ from a plain program's by a relative error of at most 0.022.
Values may be sent and summed in bfloat16 or wider, within the bound.
A program may use at most 64 MiB of HBM per device.

v0:
```python
import jax
import jax.numpy as jnp
from jax import lax
from jax.sharding import PartitionSpec as P


def gelu_tanh(values):
    return jax.nn.gelu(values, approximate=True)


def body(inputs, weight, grad_out):
    block_in = lax.all_gather(inputs, "dep", axis=0, tiled=True)
    full_weight = lax.all_gather(weight, "row", axis=0, tiled=True)
    partial_sum = jnp.dot(block_in, full_weight, preferred_element_type=jnp.float32)
    pre_act = lax.psum_scatter(
        partial_sum.astype(jnp.bfloat16), "col", scatter_dimension=0, tiled=True
    ).astype(jnp.float32)
    activation, pullback = jax.vjp(gelu_tanh, pre_act)
    hidden = activation.astype(jnp.bfloat16)
    grad_local = pullback(grad_out.astype(jnp.float32))[0].astype(jnp.bfloat16)
    grad_block = lax.all_gather(grad_local, "col", axis=0, tiled=True)
    partial_grad = lax.dot_general(
        grad_block, full_weight, (((1,), (1,)), ((), ())), preferred_element_type=jnp.float32
    )
    grad_inputs = lax.psum_scatter(
        partial_grad.astype(jnp.bfloat16), "dep", scatter_dimension=0, tiled=True
    )
    return (hidden, grad_inputs)


def solution(mesh):
    placed = (P(("row", "dep"), "col"), P(("col", "row"), "dep"), P(("row", "col"), "dep"))
    return jax.shard_map(
        body,
        mesh=mesh,
        in_specs=placed,
        out_specs=(P(("row", "col"), "dep"), P(("row", "dep"), "col")),
        check_vma=False,
    )
```

profile of v0, /device:TPU:2, one launch (start us, length us, event | category | flops | bytes accessed | tf_op | source)
XLA Modules:
  0.0 236.5 jit_solution(748125082746535518)
XLA Ops:
  7.2 0.0 all-gather.3.cloned.1.call-start
  7.2 0.7 all-gather.3.cloned.1.call-update
  7.9 0.0 reduce-scatter.3.cloned.1.call-start
  7.9 27.9 %all_gather.9 = bf16[512,768]{1,0:T(8,128)(2,1)S(1)} all-gather(bf16[64,768]{1,0:T(8,128)(2,1)} %param.3), channel_id=1, replica_groups=mesh['row'=8,'col'=8,'dep'=8] {'dep'}, dimensions={0}, use_global_device_ids=true | all-gather | bytes 884736 | tf_op jit(solution)/shard_map/all_gather | solution.py:12
  35.9 0.0 copy-start
  35.9 39.4 %all-gather.3.cloned.1.call-done = bf16[768,3072]{1,0:T(8,128)(2,1)} async-done(((bf16[96,3072]{1,0:T(8,128)(2,1)}), bf16[768,3072]{1,0:T(8,128)(2,1)}) %all-gather.3.cloned.1.call-update) | async-done | bytes 4718608 | tf_op jit(solution)/shard_map/all_gather | solution.py:13
  75.3 6.3 %convolution_convert_fusion = bf16[512,3072]{1,0:T(8,128)(2,1)} fusion(bf16[512,768]{1,0:T(8,128)(2,1)S(1)} %all_gather.9, bf16[768,3072]{1,0:T(8,128)(2,1)} %all-gather.3.cloned.1.call-done), kind=kOutput, calls=%fused_computation | convolution fusion | flops 2417491968 | bytes 8650752 | tf_op jit(solution)/shard_map/dot_general | solution.py:14
  81.6 0.0 reduce-scatter.3.cloned.1.call-update
  81.6 0.0 all-gather.5.cloned.1.call-start
  81.7 48.3 %reduce-scatter.3.cloned.1.call-done = bf16[64,3072]{1,0:T(8,128)(2,1)} async-done(((bf16[512,3072]{1,0:T(8,128)(2,1)}), bf16[64,3072]{1,0:T(8,128)(2,1)}) %reduce-scatter.3.cloned.1.call-update) | async-done | bytes 393232 | tf_op jit(solution)/shard_map/reduce_scatter | solution.py:15
  130.0 0.0 copy-done
  130.0 2.5 %fusion.3 = (bf16[64,3072]{1,0:T(8,128)(2,1)}, bf16[64,3072]{1,0:T(8,128)(2,1)}) fusion(bf16[64,3072]{1,0:T(8,128)(2,1)S(1)} %copy-done, bf16[64,3072]{1,0:T(8,128)(2,1)} %reduce-scatter.3.cloned.1.call-done), kind=kLoop, calls=%fused_computation.11 | loop fusion | flops 4718592 | bytes 1572864 | tf_op jit(solution)/shard_map/convert_element_type | solution.py:20
  132.5 0.0 all-gather.5.cloned.1.call-update
  132.5 0.0 reduce-scatter.5.cloned.1.call-start
  132.6 49.0 %all-gather.5.cloned.1.call-done = bf16[512,3072]{1,0:T(8,128)(2,1)} async-done(((bf16[64,3072]{1,0:T(8,128)(2,1)}), bf16[512,3072]{1,0:T(8,128)(2,1)}) %all-gather.5.cloned.1.call-update) | async-done | bytes 3145744 | tf_op jit(solution)/shard_map/all_gather | solution.py:21
  181.6 6.9 %convolution_convert_fusion.1 = bf16[512,768]{1,0:T(8,128)(2,1)} fusion(bf16[512,3072]{1,0:T(8,128)(2,1)} %all-gather.5.cloned.1.call-done, bf16[768,3072]{1,0:T(8,128)(2,1)} %all-gather.3.cloned.1.call-done), kind=kOutput, calls=%fused_computation.6 | convolution fusion | flops 2416312320 | bytes 8650752 | tf_op jit(solution)/shard_map/dot_general | solution.py:22
  188.5 0.0 reduce-scatter.5.cloned.1.call-update
  188.5 41.5 %reduce-scatter.5.cloned.1.call-done = bf16[64,768]{1,0:T(8,128)(2,1)} async-done(((bf16[512,768]{1,0:T(8,128)(2,1)}), bf16[64,768]{1,0:T(8,128)(2,1)}) %reduce-scatter.5.cloned.1.call-update) | async-done | bytes 98320 | tf_op jit(solution)/shard_map/reduce_scatter | solution.py:25
Async XLA Ops:
  7.2 68.2 %all-gather.3.cloned.1.call-start = ((), (), s32[]{:S(2)}) async-start(), calls=%async_computation.2 | async-start | bytes 5308416 | tf_op jit(solution)/shard_map/all_gather | solution.py:13
  7.9 122.1 %reduce-scatter.3.cloned.1.call-start = ((), (), s32[]{:S(2)}) async-start(), calls=%async_computation.3 | async-start | bytes 3538944 | tf_op jit(solution)/shard_map/reduce_scatter | solution.py:15
  35.9 94.1 %copy-start = (bf16[64,3072]{1,0:T(8,128)(2,1)S(1)}, bf16[64,3072]{1,0:T(8,128)(2,1)}, u32[]{:S(2)}) copy-start(bf16[64,3072]{1,0:T(8,128)(2,1)} %param.5) | copy-start | bytes 1179652
  81.6 100.0 %all-gather.5.cloned.1.call-start = ((), (), s32[]{:S(2)}) async-start(), calls=%async_computation.4 | async-start | bytes 3538944 | tf_op jit(solution)/shard_map/all_gather | solution.py:21
  132.5 97.5 %reduce-scatter.5.cloned.1.call-start = ((), (), s32[]{:S(2)}) async-start(), calls=%async_computation.5 | async-start | bytes 884736 | tf_op jit(solution)/shard_map/reduce_scatter | solution.py:25
Sparse Core Ops, SparseCore 0:
  10.1 65.1 all-gather.2
  81.7 48.1 reduce-scatter.2
  132.6 48.8 all-gather.4
  188.6 41.3 reduce-scatter.4
where the time goes:
time: 237 us
  waiting for transfers between devices  179 us (76%)
  blocking collectives  27.9 us (12%)
  between operations  13.8 us (6%)
  matrix products  13.2 us (6%)
  other arithmetic  2.53 us (1%)
    all_gather x1, waiting for transfers between devices, body(): grad_block = lax.all_gather(grad_local, 'col', axis=0, tiled=True)  49 us
    reduce_scatter x1, waiting for transfers between devices, body(): lax.psum_scatter(partial_sum.astype(jnp.bfloat16), 'col', scatter_dimensi...  48.3 us
    reduce_scatter x1, waiting for transfers between devices, body(): lax.psum_scatter(partial_grad.astype(jnp.bfloat16), 'dep', scatter_dimens...  41.5 us
    all_gather x1, waiting for transfers between devices, body(): full_weight = lax.all_gather(weight, 'row', axis=0, tiled=True)  39.4 us
    all_gather x1, blocking collectives, body(): block_in = lax.all_gather(inputs, 'dep', axis=0, tiled=True)  27.9 us
    dot_general x1, matrix products, body(): lax.dot_general(grad_block, full_weight, (((1,), (1,)), ((), ())), prefer...  6.91 us
    dot_general x1, matrix products, body(): jnp.dot(block_in, full_weight, preferred_element_type=jnp.float32)  6.27 us
  transfers between devices with their start and end apart: 4, of which 4 were waited for; matrix products, arithmetic and copies ran while one was open for 0% of the time, Pallas kernels for 0%

commit v1 on v0

v1 whole, which is shorter than its diff:
```python
import math

import jax
import jax.numpy as jnp
from jax import lax
from jax.experimental import pallas as pl
from jax.experimental.pallas import tpu as pltpu
from jax.sharding import PartitionSpec as P

MESH = pl.DeviceIdType.MESH
BF16, F32 = jnp.bfloat16, jnp.float32
CHUNK = 256
AHEAD = 1
NZ, NX, NY = 8, 4, 8
FWD, ACT, BWD = 5, 7, 9


def gelu_and_slope(v):
    c0 = math.sqrt(2.0 / math.pi)
    sq = v * v
    t = jnp.tanh(c0 * v * (1.0 + 0.044715 * sq))
    half = 0.5 * (1.0 + t)
    slope = half + 0.5 * v * (1.0 - t * t) * (c0 * (1.0 + 3.0 * 0.044715 * sq))
    return v * half, slope


def kernel(x_ref, w_ref, g_ref, hid_ref, out_ref, wbuf, xbuf, xsend, xrecv, gbuf, acc, ysend, yrecv, jump,
           z_ss, z_rs, sib_ss, sib_rs, own_s, f_ss, f_rs, b_ss, b_rs, h_ss, h_rs, y_ss, y_rs, j_ss, j_rs):
    n = wbuf.shape[0]
    piece, width = xbuf.shape[1], xbuf.shape[2]
    part = w_ref.shape[0]
    cut = part // 2
    row, col, y = lax.axis_index("row"), lax.axis_index("col"), lax.axis_index("dep")
    z_hi, core = row // 2, row % 2
    z_lo, x = col // 4, col % 4
    z = 2 * z_hi + z_lo

    def dev(z_, core_, x_, y_):
        return {"row": (z_ // 2) * 2 + core_, "col": (z_ % 2) * 4 + x_, "dep": y_}

    def slot(z_):
        return (z_ % 2) * 4 + z_ // 2

    up, down = dev((z + 1) % NZ, core, x, y), dev((z + 7) % NZ, core, x, y)
    sibling = dev(z, 1 - core, x, y)
    xs = [dev(z, core, (x + i) % NX, y) for i in range(1, NX)]
    ys = [dev(z, core, x, (y + i) % NY) for i in range(1, NY)]
    far = {"row": row, "col": (1 - z_lo) * 4 + x, "dep": (y + 4) % NY}
    at_home = (y // 4) == z_lo
    mine = slot(z)

    def remote(src, dst, ss, rs, to):
        return pltpu.make_async_remote_copy(src_ref=src, dst_ref=dst, send_sem=ss, recv_sem=rs, device_id=to, device_id_type=MESH)

    def cols(k):
        return pl.ds(pl.multiple_of(k * CHUNK, CHUNK), CHUNK)

    def hop(way, h, k):
        rows = pl.ds(0, part) if h < 4 else pl.ds(way * cut, cut)
        origin = (z - (h - 1) + NZ) % NZ if way == 0 else (z + (h - 1)) % NZ
        to = up if way == 0 else down
        dst = wbuf.at[k, slot(origin), core, rows]
        src = w_ref.at[:, cols(k)] if h == 1 else dst
        return remote(src, dst, z_ss.at[way, h - 1, k], z_rs.at[way, h - 1, k], to)

    def own(k):
        return pltpu.make_async_copy(w_ref.at[:, cols(k)], wbuf.at[k, mine, core], own_s.at[k])

    def to_sibling(k):
        there = wbuf.at[k, :, core]
        return remote(there, there, sib_ss.at[k], sib_rs.at[k], sibling)

    def from_sibling(k):
        there = wbuf.at[k, :, 1 - core]
        return remote(there, there, sib_ss.at[k], sib_rs.at[k], sibling)

    def fwd_copy(i, k):
        return remote(xsend.at[k, (x + i) % NX], xrecv.at[k, i - 1], f_ss.at[i - 1, k], f_rs.at[i - 1, k], xs[i - 1])

    def bwd_copy(i, k):
        return remote(gbuf.at[k, x], gbuf.at[k, x], b_ss.at[i - 1, k], b_rs.at[i - 1, k], xs[i - 1])

    def bwd_arrival(i, k):
        there = gbuf.at[k, (x + NX - i) % NX]
        return remote(there, there, b_ss.at[i - 1, k], b_rs.at[i - 1, k], xs[i - 1])

    def head_copy(i):
        return remote(xbuf.at[y], xbuf.at[y], h_ss.at[i - 1], h_rs.at[i - 1], ys[i - 1])

    def head_arrival(i):
        there = xbuf.at[(y + NY - i) % NY]
        return remote(there, there, h_ss.at[i - 1], h_rs.at[i - 1], ys[i - 1])

    barrier = pltpu.get_barrier_semaphore()
    peers = [up, down, sibling, far] + xs + ys
    for peer in peers:
        pl.semaphore_signal(barrier, inc=1, device_id=peer, device_id_type=MESH)
    pl.semaphore_wait(barrier, len(peers))

    for k in range(AHEAD):
        hop(0, 1, k).start()
        hop(1, 1, k).start()

    swap_in = remote(x_ref, xbuf.at[(y + 4) % NY], j_ss.at[0], j_rs.at[0], far)
    swap_arrival = remote(x_ref, xbuf.at[y], j_ss.at[0], j_rs.at[0], far)
    stay_in = pltpu.make_async_copy(x_ref, xbuf.at[y], j_ss.at[1])

    @pl.when(at_home)
    def _():
        stay_in.start()
        stay_in.wait()

    @pl.when(jnp.logical_not(at_home))
    def _():
        swap_in.start()

    def start_own(k, carry):
        own(k).start()
        return carry

    lax.fori_loop(0, n, start_own, 0)
    acc[...] = jnp.zeros_like(acc)

    @pl.when(jnp.logical_not(at_home))
    def _():
        swap_in.wait_send()
        swap_arrival.wait_recv()

    for i in (4, 3, 5, 2, 6, 1, 7):
        head_copy(i).start()

    def within(k, f):
        pl.when(jnp.logical_and(k >= 0, k < n))(lambda: f(k))

    def pass_on(h):
        def f(k):
            for way in (0, 1):
                hop(way, h, k).wait_recv()
                if h < 4:
                    hop(way, h + 1, k).start()
            if h == 4:
                own(k).wait()
                to_sibling(k).start()
        return f

    def send_own(k):
        hop(0, 1, k).start()
        hop(1, 1, k).start()

    def forward(k):
        @pl.when(k == 0)
        def _():
            for i in range(1, NY):
                head_arrival(i).wait_recv()
        from_sibling(k).wait_recv()
        total = None
        for h in (0, 1):
            a = xbuf[h * 4:(h + 1) * 4].reshape(4 * piece, width)
            w = wbuf[k, h * 4:(h + 1) * 4].reshape(width, CHUNK)
            term = jnp.dot(a, w, preferred_element_type=F32)
            total = term if total is None else total + term
        xsend[k] = total.astype(BF16).reshape(NX, piece, CHUNK)
        for i in (2, 1, 3):
            fwd_copy(i, k).start()

    def activate(k):
        for i in (1, 2, 3):
            fwd_copy(i, k).wait_recv()
        pre = xsend[k, x].astype(F32)
        for i in range(NX - 1):
            pre = pre + xrecv[k, i].astype(F32)
        act, slope = gelu_and_slope(pre)
        hid_ref[:, cols(k)] = act.astype(BF16)
        gbuf[k, x] = (g_ref[:, cols(k)].astype(F32) * slope).astype(BF16)
        for i in (2, 1, 3):
            bwd_copy(i, k).start()

    def backward(k):
        for i in (1, 2, 3):
            bwd_arrival(i, k).wait_recv()
        g = gbuf[k].reshape(4 * piece, CHUNK)
        for h in (0, 1):
            w = wbuf[k, h * 4:(h + 1) * 4].reshape(width, CHUNK)
            acc[h] += lax.dot_general(g, w, (((1,), (1,)), ((), ())), preferred_element_type=F32)

    def one_round(r, carry):
        for h in (4, 3, 2, 1):
            within(r - h, pass_on(h))
        within(r + AHEAD, send_own)
        within(r - FWD, forward)
        within(r - ACT, activate)
        within(r - BWD, backward)
        return carry

    lax.fori_loop(0, n + BWD, one_round, 0)

    half = piece // 2

    def own_rows(p, sub):
        return acc[p // 4, pl.ds(pl.multiple_of((p % 4) * piece + sub * half, half), half)]

    def y_copy(way, h, sub):
        rows = pl.ds(sub * half, half)
        to = ys[0] if way == 0 else ys[NY - 2]
        return remote(ysend.at[way, h - 1, rows], yrecv.at[way, h - 1, rows], y_ss.at[way, h - 1, sub], y_rs.at[way, h - 1, sub], to)

    for h in (1, 2, 3, 4):
        for order in (0, 1):
            for way in (0, 1):
                sub = order if way == 0 else 1 - order
                if h == 1 and order == 1:
                    continue
                p = (y + 5 - h) % NY if way == 0 else (y + h + 3) % NY
                rows = pl.ds(sub * half, half)
                value = own_rows(p, sub)
                if h > 2 or (h == 2 and order == 0):
                    y_copy(way, h - 1, sub).wait_recv()
                    value = value + yrecv[way, h - 2, rows].astype(F32)
                ysend[way, h - 1, rows] = value.astype(BF16)
                y_copy(way, h, sub).start()
    for sub in (0, 1):
        rows = pl.ds(sub * half, half)
        value = own_rows(y, sub)
        for way in (0, 1):
            y_copy(way, 4, sub).wait_recv()
            value = value + yrecv[way, 3, rows].astype(F32)
        jump[rows] = value.astype(BF16)
    swap_out = remote(jump, out_ref, j_ss.at[2], j_rs.at[1], far)

    @pl.when(jnp.logical_not(at_home))
    def _():
        swap_out.start()
        swap_out.wait()

    @pl.when(at_home)
    def _():
        out_ref[...] = jump[...]

    def drain(k, carry):
        for way in (0, 1):
            for h in (1, 2, 3, 4):
                hop(way, h, k).wait_send()
        to_sibling(k).wait_send()
        for i in (1, 2, 3):
            fwd_copy(i, k).wait_send()
            bwd_copy(i, k).wait_send()
        return carry

    lax.fori_loop(0, n, drain, 0)
    for i in range(1, NY):
        head_copy(i).wait_send()
    for way in (0, 1):
        for h in (1, 2, 3, 4):
            for sub in (0, 1):
                if h > 1 or sub == way:
                    y_copy(way, h, sub).wait_send()


def body(inputs, weight, grad_out):
    piece, width = inputs.shape
    part, units = weight.shape
    n = units // CHUNK
    dma = pltpu.SemaphoreType.DMA
    vmem = pl.BlockSpec(memory_space=pltpu.VMEM)
    return pl.pallas_call(
        kernel,
        out_shape=(jax.ShapeDtypeStruct((piece, units), BF16), jax.ShapeDtypeStruct((piece, width), BF16)),
        in_specs=[pl.BlockSpec(memory_space=pl.ANY), pl.BlockSpec(memory_space=pl.ANY), vmem],
        out_specs=(vmem, vmem),
        scratch_shapes=[
            pltpu.VMEM((n, NZ, 2, part, CHUNK), BF16),
            pltpu.VMEM((NY, piece, width), BF16),
            pltpu.VMEM((n, NX, piece, CHUNK), BF16),
            pltpu.VMEM((n, NX - 1, piece, CHUNK), BF16),
            pltpu.VMEM((n, NX, piece, CHUNK), BF16),
            pltpu.VMEM((2, 4 * piece, width), F32),
            pltpu.VMEM((2, 4, piece, width), BF16),
            pltpu.VMEM((2, 4, piece, width), BF16),
            pltpu.VMEM((piece, width), BF16),
            dma((2, 4, n)), dma((2, 4, n)), dma((n,)), dma((n,)), dma((n,)),
            dma((3, n)), dma((3, n)), dma((3, n)), dma((3, n)),
            dma((NY - 1,)), dma((NY - 1,)), dma((2, 4, 2)), dma((2, 4, 2)), dma((3,)), dma((2,)),
        ],
        compiler_params=pltpu.CompilerParams(collective_id=0, has_side_effects=True, vmem_limit_bytes=48 << 20),
        name="up_projection",
    )(inputs, weight, grad_out)


def solution(mesh):
    return jax.shard_map(
        body,
        mesh=mesh,
        in_specs=(P(("row", "dep"), "col"), P(("col", "row"), "dep"), P(("row", "col"), "dep")),
        out_specs=(P(("row", "col"), "dep"), P(("row", "dep"), "col")),
        check_vma=False,
    )
```

time: 237 us -> 128 us (0.54)
  the two profiles are of different devices: /device:TPU:2 before, /device:TPU:64 now
where the time goes in v1:
time: 128 us
  Pallas kernels  123 us (96%)
  local copies, waits for them, and re-layouts  4.33 us (3%)
    pallas_call x1, Pallas kernels, body(): pl.pallas_call(kernel, out_shape=(jax.ShapeDtypeStruct((piece, units), BF...  123 us
    unnamed x8, local copies, waits for them, and re-layouts  4.33 us

profile of v1, /device:TPU:64, one launch (start us, length us, event | category | flops | bytes accessed | tf_op | source)
XLA Modules:
  0.0 127.6 jit_solution(16929912902946129068)
XLA Ops:
  0.6 0.0 copy-start
  0.6 1.1 copy-done
  1.7 0.0 copy-start.1
  1.7 1.0 copy-done.1
  2.7 0.0 copy-start.2
  2.7 0.9 copy-done.2
  3.6 122.6 %up_projection.1 = (bf16[64,3072]{1,0:T(8,128)(2,1)S(1)}, bf16[64,768]{1,0:T(8,128)(2,1)S(1)}) custom-call(bf16[64,768]{1,0:T(8,128)(2,1)S(1)} %copy-done.2, bf16[96,3072]{1,0:T(8,128)(2,1)S(1)} %copy-done, bf16[64,3072]{1,0:T(8,128)(2,1)S(1)} %copy-done.1), custom_call_target="tpu_custom_call" | custom-call | tf_op jit(solution)/shard_map/up_projection/pallas_call | solution.py:265
  126.2 0.7 copy.7
  126.9 0.6 copy.8
Async XLA Ops:
  0.6 1.1 copy-start
  1.7 1.0 copy-start.1
  2.7 0.9 copy-start.2

commit v2 on v1

v2 whole, which is shorter than its diff:
```python
import math

import jax
import jax.numpy as jnp
from jax import lax
from jax.experimental import pallas as pl
from jax.experimental.pallas import tpu as pltpu
from jax.sharding import PartitionSpec as P

MESH = pl.DeviceIdType.MESH
BF16, F32 = jnp.bfloat16, jnp.float32
CHUNK = 256
HOPS = (1, 3, 5, 7)
ORDER = (4, 3, 2, 1)
AHEAD = 2
NZ, NX, NY = 8, 4, 8
FWD, ACT, BWD = 8, 10, 12
SWAP, SPREAD = 2, 6
HELD = 1


def gelu_and_slope(v):
    c0 = math.sqrt(2.0 / math.pi)
    sq = v * v
    t = jnp.tanh(c0 * v * (1.0 + 0.044715 * sq))
    half = 0.5 * (1.0 + t)
    slope = half + 0.5 * v * (1.0 - t * t) * (c0 * (1.0 + 3.0 * 0.044715 * sq))
    return v * half, slope


def kernel(x_ref, w_ref, g_ref, hid_ref, out_ref, wbuf, xbuf, xsend, xrecv, gbuf, acc, ysend, yrecv, yrelay, total, gout,
           z_ss, z_rs, sib_ss, sib_rs, own_s, f_ss, f_rs, b_ss, b_rs, h_ss, h_rs, y_ss, y_rs, r_ss, r_rs, j_ss, j_rs, g_s, last_ss, last_rs):
    n = wbuf.shape[0]
    piece, width = xbuf.shape[1], xbuf.shape[2]
    part = w_ref.shape[0]
    cut = part // 2
    row, col, y = lax.axis_index("row"), lax.axis_index("col"), lax.axis_index("dep")
    z_hi, core = row // 2, row % 2
    z_lo, x = col // 4, col % 4
    z = 2 * z_hi + z_lo

    def dev(z_, core_, x_, y_):
        return {"row": (z_ // 2) * 2 + core_, "col": (z_ % 2) * 4 + x_, "dep": y_}

    def slot(z_):
        return (z_ % 2) * 4 + z_ // 2

    up, down = dev((z + 1) % NZ, core, x, y), dev((z + 7) % NZ, core, x, y)
    up_other, down_other = dev((z + 1) % NZ, 1 - core, x, y), dev((z + 7) % NZ, 1 - core, x, y)
    sibling = dev(z, 1 - core, x, y)
    xs = [dev(z, core, (x + i) % NX, y) for i in range(1, NX)]
    ys = {i: dev(z, core, x, (y + i + NY) % NY) for i in (1, -1, 2, -2)}
    far = {"row": row, "col": (1 - z_lo) * 4 + x, "dep": (y + 4) % NY}
    at_home = (y // 4) == z_lo

    def flipped(i):
        return {"row": row, "col": (1 - z_lo) * 4 + x, "dep": (y + i + NY) % NY}

    mine = slot(z)

    def remote(src, dst, ss, rs, to):
        return pltpu.make_async_remote_copy(src_ref=src, dst_ref=dst, send_sem=ss, recv_sem=rs, device_id=to, device_id_type=MESH)

    def cols(k):
        return pl.ds(pl.multiple_of(k * CHUNK, CHUNK), CHUNK)

    def hop(way, h, k):
        rows = pl.ds(0, part) if h < 4 else pl.ds(way * cut, cut)
        origin = (z - (h - 1) + NZ) % NZ if way == 0 else (z + (h - 1)) % NZ
        to = up if way == 0 else down
        dst = wbuf.at[k, slot(origin), core, rows]
        src = w_ref.at[:, cols(k)] if h == 1 else dst
        return remote(src, dst, z_ss.at[way, h - 1, k], z_rs.at[way, h - 1, k], to)

    def own(k):
        return pltpu.make_async_copy(w_ref.at[:, cols(k)], wbuf.at[k, mine, core], own_s.at[k])

    def to_sibling(k):
        there = wbuf.at[k, :, core]
        return remote(there, there, sib_ss.at[k], sib_rs.at[k], sibling)

    def from_sibling(k):
        there = wbuf.at[k, :, 1 - core]
        return remote(there, there, sib_ss.at[k], sib_rs.at[k], sibling)

    def one_to_sibling(away):
        there = wbuf.at[n - 1, slot((z + away + NZ) % NZ), core]
        return remote(there, there, last_ss.at[away + 3], last_rs.at[away + 3], sibling)

    def one_from_sibling(away):
        there = wbuf.at[n - 1, slot((z + away + NZ) % NZ), 1 - core]
        return remote(there, there, last_ss.at[away + 3], last_rs.at[away + 3], sibling)

    def last_hop(way):
        origin = (z + (5, 3)[way]) % NZ
        there = wbuf.at[n - 1, slot(origin), core, pl.ds(way * cut, cut)]
        return remote(there, there, last_ss.at[7 + way], last_rs.at[7 + way], (up_other, down_other)[way])

    def last_hop_arrival(way):
        there = wbuf.at[n - 1, slot((z + 4) % NZ), 1 - core, pl.ds(way * cut, cut)]
        return remote(there, there, last_ss.at[7 + way], last_rs.at[7 + way], (up_other, down_other)[way])

    x_half = piece // 2
    halves = (pl.ds(0, x_half), pl.ds(x_half, x_half))

    def fwd_copy(i, k):
        return remote(xsend.at[k, (x + i) % NX], xrecv.at[k, i - 1], f_ss.at[i - 1, k], f_rs.at[i - 1, k], xs[i - 1])

    def bwd_copy(i, k):
        return remote(gbuf.at[k, x], gbuf.at[k, x], b_ss.at[i - 1, k], b_rs.at[i - 1, k], xs[i - 1])

    def bwd_arrival(i, k):
        there = gbuf.at[k, (x + NX - i) % NX]
        return remote(there, there, b_ss.at[i - 1, k], b_rs.at[i - 1, k], xs[i - 1])

    def head_near(i, step, src):
        return remote(src, xbuf.at[y], h_ss.at[i], h_rs.at[i], ys[step])

    def head_near_arrival(i, step):
        there = xbuf.at[(y - step + NY) % NY]
        return remote(there, there, h_ss.at[i], h_rs.at[i], ys[step])

    NEAR = ((0, 2), (1, -2), (2, 1), (3, -1))

    def head_on(i, step, rows, origin):
        there = xbuf.at[(y + origin + NY) % NY, rows]
        return remote(there, there, h_ss.at[i], h_rs.at[i], ys[step])

    whole = pl.ds(0, piece)
    ON = ((4, 2, halves[0], -2), (5, -2, halves[1], 2), (6, 1, whole, -2), (7, -1, whole, 2))

    def head_on_arrival(i, step, rows, origin):
        there = xbuf.at[(y + origin - step + NY) % NY, rows]
        return remote(there, there, h_ss.at[i], h_rs.at[i], ys[step])

    barrier = pltpu.get_barrier_semaphore()
    same = [up, down, far] + xs + list(ys.values()) + [flipped(i) for i in (1, -1, 2, -2)]
    across = [sibling, up_other, down_other]
    for peer in same:
        pl.semaphore_signal(barrier, inc=1, device_id=peer, device_id_type=MESH)

    @pl.when(core == 0)
    def _():
        pl.semaphore_wait(barrier, len(same))

    @pl.when(core == 1)
    def _():
        pl.semaphore_wait(barrier, len(same) + len(across))

    for peer in across:
        pl.semaphore_signal(barrier, inc=1, device_id=peer, device_id_type=MESH)

    for k in range(AHEAD):
        hop(0, 1, k).start()
        hop(1, 1, k).start()

    swap_in = remote(x_ref, xbuf.at[(y + 4) % NY], j_ss.at[0], j_rs.at[0], far)
    swap_arrival = remote(x_ref, xbuf.at[y], j_ss.at[0], j_rs.at[0], far)
    stay_in = pltpu.make_async_copy(x_ref, xbuf.at[y], j_ss.at[1])

    @pl.when(at_home)
    def _():
        for i, step in NEAR:
            head_near(i, step, x_ref).start()
        stay_in.start()

    @pl.when(jnp.logical_not(at_home))
    def _():
        swap_in.start()

    def start_own(k, carry):
        own(k).start()
        return carry

    lax.fori_loop(0, n, start_own, 0)
    load_g = pltpu.make_async_copy(g_ref, gout, g_s)
    load_g.start()
    acc[...] = jnp.zeros_like(acc)

    def swapped():
        @pl.when(jnp.logical_not(at_home))
        def _():
            swap_arrival.wait_recv()
            for i, step in NEAR:
                head_near(i, step, xbuf.at[y]).start()

    def spread():
        for i, step in NEAR[:2]:
            head_near_arrival(i, step).wait_recv()
        for way in ON:
            head_on(*way).start()

    def within(k, f):
        pl.when(jnp.logical_and(k >= 0, k < n))(lambda: f(k))

    def pass_on(h):
        def f(k):
            for way in (0, 1):
                hop(way, h, k).wait_recv()
                if h < 4:
                    hop(way, h + 1, k).start()
                if h == 3:
                    pl.when(k == n - 1)(last_hop(way).start)
                if h < 4:
                    pl.when(k == n - 1)(one_to_sibling(h if way else -h).start)
            if h == 1:
                own(k).wait()
                pl.when(k == n - 1)(one_to_sibling(0).start)
            if h == 4:
                @pl.when(jnp.logical_and(core == 0, k == 0))
                def _():
                    pl.semaphore_wait(barrier, len(across))

                pl.when(k < n - 1)(to_sibling(k).start)
        return f

    def send_own(k):
        hop(0, 1, k).start()
        hop(1, 1, k).start()

    def forward(k):
        @pl.when(k == 0)
        def _():
            pl.when(at_home)(stay_in.wait)
            for i, step in NEAR[2:]:
                head_near_arrival(i, step).wait_recv()
            for way in ON:
                head_on_arrival(*way).wait_recv()
        pl.when(k < n - 1)(from_sibling(k).wait_recv)

        @pl.when(k == n - 1)
        def _():
            for away in range(-3, 4):
                one_from_sibling(away).wait_recv()
            for way in (0, 1):
                last_hop_arrival(way).wait_recv()

        partial = None
        for h in (0, 1):
            a = xbuf[h * 4:(h + 1) * 4].reshape(4 * piece, width)
            w = wbuf[k, h * 4:(h + 1) * 4].reshape(width, CHUNK)
            term = jnp.dot(a, w, preferred_element_type=F32)
            partial = term if partial is None else partial + term
        xsend[k] = partial.astype(BF16).reshape(NX, piece, CHUNK)

        for i in (2, 1, 3):
            fwd_copy(i, k).start()

    def activate(k):
        pl.when(k == 0)(load_g.wait)
        pre = xsend[k, x].astype(F32)
        for i in (1, 2, 3):
            fwd_copy(i, k).wait_recv()
            pre = pre + xrecv[k, i - 1].astype(F32)
        act, slope = gelu_and_slope(pre)
        gbuf[k, x] = (gout[:, cols(k)].astype(F32) * slope).astype(BF16)
        for i in (2, 1, 3):
            bwd_copy(i, k).start()
        hid_ref[:, cols(k)] = act.astype(BF16)

    def backward(k):
        for i in (1, 2, 3):
            bwd_arrival(i, k).wait_recv()
        g = gbuf[k].reshape(4 * piece, CHUNK)
        for h in (0, 1):
            w = wbuf[k, h * 4:(h + 1) * 4].reshape(width, CHUNK)
            acc[h] += lax.dot_general(g, w, (((1,), (1,)), ((), ())), preferred_element_type=F32)

    def stage(r, lag, f):
        @pl.when(r == lag + HELD)
        def _():
            lax.fori_loop(0, HELD, lambda k, carry: (f(k), carry)[1], 0)

        @pl.when(jnp.logical_and(r >= lag + HELD, r < lag + n))
        def _():
            f(r - lag)

    def one_round(r, carry):
        for h in ORDER:
            within(r - HOPS[h - 1], pass_on(h))
        within(r + AHEAD, send_own)
        pl.when(r == SWAP)(swapped)
        pl.when(r == SPREAD)(spread)
        stage(r, FWD, forward)
        stage(r, ACT, activate)
        stage(r, BWD, backward)
        return carry

    lax.fori_loop(0, n + BWD, one_round, 0)

    for h in (0, 1):
        for p in range(4):
            ysend[h * 4 + p] = acc[h, p * piece:(p + 1) * piece].astype(BF16)

    def ring(step, flip):
        return {"row": row, "col": (1 - z_lo if flip else z_lo) * 4 + x, "dep": (y + step + NY) % NY}

    def held(away, flip):
        return ((1 - z_lo if flip else z_lo) * 4 + (y + away + NY) % 4)

    def here(away):
        return ((y + away + NY) % NY) // 4 == z_lo

    first, second = (halves[1], halves[0]), (halves[0], halves[1])
    TO_RELAY = ((-3, -1, first[0], 3, 3), (3, 1, first[1], 4, 4), (-2, 0, whole, 7, 7), (2, 0, whole, 8, 8),
                (-3, -1, second[0], 3, 9), (3, 1, second[1], 4, 10), (-4, -2, second[0], 5, 5), (4, 2, second[1], 6, 6))
    TO_TARGET = ((-1, -1, whole, 0, 0), (1, 1, whole, 1, 1), (0, 0, whole, 2, 2))

    def term(away, step, rows, at, sem, flip):
        return remote(ysend.at[held(away, flip), rows], yrecv.at[at, rows], y_ss.at[sem, flip], y_rs.at[sem], ring(step, flip))

    def each_term(terms, act):
        for t in terms:
            for flip in (0, 1):
                if t[1] or flip:
                    pl.when(here(t[0]))(lambda t=t, flip=flip: act(term(*t, flip)))

    each_term(TO_RELAY, lambda copy: copy.start())

    def arrived(at, rows, sem):
        there = yrecv.at[at, rows]
        remote(there, there, y_ss.at[sem, 0], y_rs.at[sem], ring(1, 0)).wait_recv()
        return yrecv[at, rows].astype(F32)

    def relayed(way, rows, sem):
        return remote(yrelay.at[way, rows], yrecv.at[9 + way, rows], r_ss.at[way, sem], r_rs.at[way, sem], ring((-2, 2)[way], 0))

    for way in (0, 1):
        away = (-2, 2)[way]

        @pl.when(here(away))
        def _():
            yrelay[way] = ysend[held(away, 0)]

        @pl.when(jnp.logical_not(here(away)))
        def _():
            yrelay[way] = arrived(7 + way, whole, 7 + way).astype(BF16)

        there = yrelay.at[way, first[way]]
        there[...] = (there[...].astype(F32) + arrived(3 + way, first[way], 3 + way)).astype(BF16)
        relayed(way, first[way], 0).start()

    each_term(TO_TARGET, lambda copy: copy.start())

    for way in (0, 1):
        there = yrelay.at[way, second[way]]
        there[...] = (there[...].astype(F32) + arrived(3 + way, second[way], 9 + way) + arrived(5 + way, second[way], 5 + way)).astype(BF16)
        relayed(way, second[way], 1).start()

    @pl.when(at_home)
    def _():
        total[...] = ysend[held(0, 0)].astype(F32)

    @pl.when(jnp.logical_not(at_home))
    def _():
        total[...] = arrived(2, whole, 2)

    total[...] += arrived(0, whole, 0) + arrived(1, whole, 1)
    for sem, rows in ((0, first), (1, second)):
        for way in (0, 1):
            relayed(way, rows[way], sem).wait_recv()
            total[rows[way]] += yrecv[9 + way, rows[way]].astype(F32)
    out_ref[...] = total[...].astype(BF16)

    def drain(k, carry):
        for way in (0, 1):
            for h in (1, 2, 3, 4):
                hop(way, h, k).wait_send()
        pl.when(k < n - 1)(to_sibling(k).wait_send)
        for i in (1, 2, 3):
            fwd_copy(i, k).wait_send()
            bwd_copy(i, k).wait_send()
        return carry

    lax.fori_loop(0, n, drain, 0)
    for away in range(-3, 4):
        one_to_sibling(away).wait_send()
    for way in (0, 1):
        last_hop(way).wait_send()
    pl.when(jnp.logical_not(at_home))(swap_in.wait_send)
    for i, step in NEAR:
        head_near(i, step, x_ref).wait_send()
    for way in ON:
        head_on(*way).wait_send()
    each_term(TO_RELAY + TO_TARGET, lambda copy: copy.wait_send())
    for way in (0, 1):
        relayed(way, first[way], 0).wait_send()
        relayed(way, second[way], 1).wait_send()


def body(inputs, weight, grad_out):
    piece, width = inputs.shape
    part, units = weight.shape
    n = units // CHUNK
    dma = pltpu.SemaphoreType.DMA
    vmem = pl.BlockSpec(memory_space=pltpu.VMEM)
    return pl.pallas_call(
        kernel,
        out_shape=(jax.ShapeDtypeStruct((piece, units), BF16), jax.ShapeDtypeStruct((piece, width), BF16)),
        in_specs=[pl.BlockSpec(memory_space=pl.ANY)] * 3,
        out_specs=(vmem, vmem),
        scratch_shapes=[
            pltpu.VMEM((n, NZ, 2, part, CHUNK), BF16),
            pltpu.VMEM((NY, piece, width), BF16),
            pltpu.VMEM((n, NX, piece, CHUNK), BF16),
            pltpu.VMEM((n, NX - 1, piece, CHUNK), BF16),
            pltpu.VMEM((n, NX, piece, CHUNK), BF16),
            pltpu.VMEM((2, 4 * piece, width), F32),
            pltpu.VMEM((8, piece, width), BF16),
            pltpu.VMEM((11, piece, width), BF16),
            pltpu.VMEM((2, piece, width), BF16),
            pltpu.VMEM((piece, width), F32),
            pltpu.VMEM((piece, units), BF16),
            dma((2, 4, n)), dma((2, 4, n)), dma((n,)), dma((n,)), dma((n,)),
            dma((3, n)), dma((3, n)), dma((3, n)), dma((3, n)),
            dma((8,)), dma((8,)), dma((11, 2)), dma((11,)), dma((2, 2)), dma((2, 2)), dma((2,)), dma((1,)), dma, dma((9,)), dma((9,)),
        ],
        compiler_params=pltpu.CompilerParams(collective_id=0, has_side_effects=True, vmem_limit_bytes=60 << 20),
        name="up_projection",
    )(inputs, weight, grad_out)


def solution(mesh):
    return jax.shard_map(
        body,
        mesh=mesh,
        in_specs=(P(("row", "dep"), "col"), P(("col", "row"), "dep"), P(("row", "col"), "dep")),
        out_specs=(P(("row", "col"), "dep"), P(("row", "dep"), "col")),
        check_vma=False,
    )
```

time: 128 us -> 109 us (0.85)
  the two profiles are of different devices: /device:TPU:64 before, /device:TPU:2 now
where the time goes in v2:
time: 109 us
  Pallas kernels  106 us (97%)
  local copies, waits for them, and re-layouts  2.45 us (2%)
    pallas_call x1, Pallas kernels, body(): pl.pallas_call(kernel, out_shape=(jax.ShapeDtypeStruct((piece, units), BF...  106 us
    unnamed x4, local copies, waits for them, and re-layouts  2.45 us

profile of v2, /device:TPU:2, one launch (start us, length us, event | category | flops | bytes accessed | tf_op | source)
XLA Modules:
  0.0 109.3 jit_solution(3358378207299744297)
XLA Ops:
  0.6 106.2 %up_projection.1 = (bf16[64,3072]{1,0:T(8,128)(2,1)}, bf16[64,768]{1,0:T(8,128)(2,1)}) custom-call(bf16[64,768]{1,0:T(8,128)(2,1)} %x_ref.1, bf16[96,3072]{1,0:T(8,128)(2,1)} %w_ref.1, bf16[64,3072]{1,0:T(8,128)(2,1)} %g_ref.1), custom_call_target="tpu_custom_call" | custom-call | tf_op jit(solution)/shard_map/up_projection/pallas_call | solution.py:397
  106.8 0.0 copy-start
  106.8 1.8 %copy.7 = bf16[64,3072]{1,0:T(8,128)(2,1)} copy(bf16[64,3072]{1,0:T(8,128)(2,1)} %get-tuple-element.4) | data formatting | bytes 786432
  108.6 0.0 copy-done
  108.7 0.6 copy.8
Async XLA Ops:
  106.8 1.8 %copy-start = (bf16[64,768]{1,0:T(8,128)(2,1)S(1)}, bf16[64,768]{1,0:T(8,128)(2,1)}, u32[]{:S(2)}) copy-start(bf16[64,768]{1,0:T(8,128)(2,1)} %get-tuple-element.5) | copy-start | bytes 294916

commit v3 on v2

--- a/solution.py
+++ b/solution.py
@@ -14,6 +14,7 @@
 ORDER = (4, 3, 2, 1)
 AHEAD = 2
 NZ, NX, NY = 8, 4, 8
+VMEM = 55783424
 FWD, ACT, BWD = 8, 10, 12
 SWAP, SPREAD = 2, 6
 HELD = 1
@@ -415,7 +416,7 @@
             dma((3, n)), dma((3, n)), dma((3, n)), dma((3, n)),
             dma((8,)), dma((8,)), dma((11, 2)), dma((11,)), dma((2, 2)), dma((2, 2)), dma((2,)), dma((1,)), dma, dma((9,)), dma((9,)),
         ],
-        compiler_params=pltpu.CompilerParams(collective_id=0, has_side_effects=True, vmem_limit_bytes=60 << 20),
+        compiler_params=pltpu.CompilerParams(collective_id=0, has_side_effects=True, vmem_limit_bytes=VMEM),
         name="up_projection",
     )(inputs, weight, grad_out)
 

time: 109 us -> 108 us (level)
    pallas_call x1, Pallas kernels: 106 us -> 105 us  [body(): pl.pallas_call(kernel, out_shape=(jax.ShapeDtypeStruct((piece, units), BF...]
where the time goes in v3:
time: 108 us
  Pallas kernels  105 us (97%)
  local copies, waits for them, and re-layouts  2.27 us (2%)
    pallas_call x1, Pallas kernels, body(): pl.pallas_call(kernel, out_shape=(jax.ShapeDtypeStruct((piece, units), BF...  105 us
    unnamed x4, local copies, waits for them, and re-layouts  2.27 us

profile of v3, /device:TPU:2, one launch (start us, length us, event | category | flops | bytes accessed | tf_op | source)
XLA Modules:
  0.0 107.8 jit_solution(3254913931843397252)
XLA Ops:
  0.6 0.0 copy-start
  0.6 0.9 copy-done
  1.5 104.9 %up_projection.1 = (bf16[64,3072]{1,0:T(8,128)(2,1)S(1)}, bf16[64,768]{1,0:T(8,128)(2,1)S(1)}) custom-call(bf16[64,768]{1,0:T(8,128)(2,1)S(1)} %copy-done, bf16[96,3072]{1,0:T(8,128)(2,1)} %w_ref.1, bf16[64,3072]{1,0:T(8,128)(2,1)} %g_ref.1), custom_call_target="tpu_custom_call" | custom-call | tf_op jit(solution)/shard_map/up_projection/pallas_call | solution.py:398
  106.4 0.7 copy.7
  107.2 0.6 copy.8
Async XLA Ops:
  0.6 0.9 copy-start

commit v4 on v3

--- a/solution.py
+++ b/solution.py
@@ -15,7 +15,7 @@
 AHEAD = 2
 NZ, NX, NY = 8, 4, 8
 VMEM = 55783424
-FWD, ACT, BWD = 8, 10, 12
+FWD, ACT, BWD = 8, 9, 11
 SWAP, SPREAD = 2, 6
 HELD = 1
 
@@ -305,7 +305,7 @@
     first, second = (halves[1], halves[0]), (halves[0], halves[1])
     TO_RELAY = ((-3, -1, first[0], 3, 3), (3, 1, first[1], 4, 4), (-2, 0, whole, 7, 7), (2, 0, whole, 8, 8),
                 (-3, -1, second[0], 3, 9), (3, 1, second[1], 4, 10), (-4, -2, second[0], 5, 5), (4, 2, second[1], 6, 6))
-    TO_TARGET = ((-1, -1, whole, 0, 0), (1, 1, whole, 1, 1), (0, 0, whole, 2, 2))
+    OVER_Z = ((-1, 0, whole, 11, 11), (1, 0, whole, 12, 12), (0, 0, whole, 2, 2))
 
     def term(away, step, rows, at, sem, flip):
         return remote(ysend.at[held(away, flip), rows], yrecv.at[at, rows], y_ss.at[sem, flip], y_rs.at[sem], ring(step, flip))
@@ -316,7 +316,7 @@
                 if t[1] or flip:
                     pl.when(here(t[0]))(lambda t=t, flip=flip: act(term(*t, flip)))
 
-    each_term(TO_RELAY, lambda copy: copy.start())
+    each_term(TO_RELAY + OVER_Z, lambda copy: copy.start())
 
     def arrived(at, rows, sem):
         there = yrecv.at[at, rows]
@@ -341,12 +341,24 @@
         there[...] = (there[...].astype(F32) + arrived(3 + way, first[way], 3 + way)).astype(BF16)
         relayed(way, first[way], 0).start()
 
-    each_term(TO_TARGET, lambda copy: copy.start())
+    def to_next(way, passed):
+        src = yrecv.at[11 + way] if passed else ysend.at[held((-1, 1)[way], 0)]
+        return remote(src, yrecv.at[way], y_ss.at[way, 0], y_rs.at[way], ring((-1, 1)[way], 0))
+
+    for way in (0, 1):
+        pl.when(here((-1, 1)[way]))(to_next(way, False).start)
 
     for way in (0, 1):
         there = yrelay.at[way, second[way]]
         there[...] = (there[...].astype(F32) + arrived(3 + way, second[way], 9 + way) + arrived(5 + way, second[way], 5 + way)).astype(BF16)
         relayed(way, second[way], 1).start()
+
+    for way in (0, 1):
+        @pl.when(jnp.logical_not(here((-1, 1)[way])))
+        def _():
+            there = yrecv.at[11 + way]
+            remote(there, there, y_ss.at[11 + way, 0], y_rs.at[11 + way], ring(1, 0)).wait_recv()
+            to_next(way, True).start()
 
     @pl.when(at_home)
     def _():
@@ -383,7 +395,9 @@
         head_near(i, step, x_ref).wait_send()
     for way in ON:
         head_on(*way).wait_send()
-    each_term(TO_RELAY + TO_TARGET, lambda copy: copy.wait_send())
+    each_term(TO_RELAY + OVER_Z, lambda copy: copy.wait_send())
+    for way in (0, 1):
+        to_next(way, True).wait_send()
     for way in (0, 1):
         relayed(way, first[way], 0).wait_send()
         relayed(way, second[way], 1).wait_send()
@@ -408,13 +422,13 @@
             pltpu.VMEM((n, NX, piece, CHUNK), BF16),
             pltpu.VMEM((2, 4 * piece, width), F32),
             pltpu.VMEM((8, piece, width), BF16),
-            pltpu.VMEM((11, piece, width), BF16),
+            pltpu.VMEM((13, piece, width), BF16),
             pltpu.VMEM((2, piece, width), BF16),
             pltpu.VMEM((piece, width), F32),
             pltpu.VMEM((piece, units), BF16),
             dma((2, 4, n)), dma((2, 4, n)), dma((n,)), dma((n,)), dma((n,)),
             dma((3, n)), dma((3, n)), dma((3, n)), dma((3, n)),
-            dma((8,)), dma((8,)), dma((11, 2)), dma((11,)), dma((2, 2)), dma((2, 2)), dma((2,)), dma((1,)), dma, dma((9,)), dma((9,)),
+            dma((8,)), dma((8,)), dma((13, 2)), dma((13,)), dma((2, 2)), dma((2, 2)), dma((2,)), dma((1,)), dma, dma((9,)), dma((9,)),
         ],
         compiler_params=pltpu.CompilerParams(collective_id=0, has_side_effects=True, vmem_limit_bytes=VMEM),
         name="up_projection",

time: 108 us -> 106 us (0.981)
  Pallas kernels: 105 us -> 103 us
    pallas_call x1, Pallas kernels: 105 us -> 103 us  [body(): pl.pallas_call(kernel, out_shape=(jax.ShapeDtypeStruct((piece, units), BF...]
where the time goes in v4:
time: 106 us
  Pallas kernels  103 us (97%)
  local copies, waits for them, and re-layouts  2.27 us (2%)
    pallas_call x1, Pallas kernels, body(): pl.pallas_call(kernel, out_shape=(jax.ShapeDtypeStruct((piece, units), BF...  103 us
    unnamed x4, local copies, waits for them, and re-layouts  2.27 us

profile of v4, /device:TPU:2, one launch (start us, length us, event | category | flops | bytes accessed | tf_op | source)
XLA Modules:
  0.0 105.9 jit_solution(3412034459814477514)
XLA Ops:
  0.6 0.0 copy-start
  0.6 0.9 copy-done
  1.5 103.0 %up_projection.1 = (bf16[64,3072]{1,0:T(8,128)(2,1)S(1)}, bf16[64,768]{1,0:T(8,128)(2,1)S(1)}) custom-call(bf16[64,768]{1,0:T(8,128)(2,1)S(1)} %copy-done, bf16[96,3072]{1,0:T(8,128)(2,1)} %w_ref.1, bf16[64,3072]{1,0:T(8,128)(2,1)} %g_ref.1), custom_call_target="tpu_custom_call" | custom-call | tf_op jit(solution)/shard_map/up_projection/pallas_call | solution.py:412
  104.5 0.7 copy.7
  105.3 0.6 copy.8
Async XLA Ops:
  0.6 0.9 copy-start
